TPU v7x, 128 devices: a whole 4x4x4 slice. The times are simulated.
128 devices in a mesh: node: 16 (over z_hi, x, core), group: 8 (over z_lo, y).
Axes of the slice: x: 4, y: 4, z: 4 (z_hi: 2, z_lo: 2; z = z_hi * 2 + z_lo), core: 2. Of those that a mesh axis runs over, the one named last changes fastest.
Arguments:
- tokens: bfloat16 [49152, 5120], P(('node', 'group')), may hold values from -24 to 24
- w_codes: bfloat16 [5120, 2048], P('node'), may hold values from -4 to 4
- w_scale: bfloat16 [5120, 16], P('node'), may hold values from 0.0048828125 to 0.0390625
- gain: float32 [1024], replicated, may hold values from 0.5 to 1.5
- key_cot: bfloat16 [49152, 1024], P(('node', 'group')), may hold values from -8 to 8
- value_cot: bfloat16 [49152, 1024], P(('node', 'group')), may hold values from -6 to 6
- grad_scale: float32 [5120, 16], replicated, may hold values from 39.191837 to 391.91837
Outputs:
- keys: bfloat16 [49152, 1024], P(('node', 'group'))
- values: bfloat16 [49152, 1024], P(('node', 'group'))
- grad_tokens: bfloat16 [49152, 5120], P(('node', 'group'))
- grad_codes: float32 [5120, 2048], P(('node', 'group'))
- grad_gain: float32 [1024], replicated
All inputs are finite; a program needn't handle non-finite values.
Results may differ from a plain program's by a relative error of at most 0.027.
Values may be sent and summed in bfloat16 or wider, within the bound.
No kernel may reach another device: no remote copies, remote signals or barrier semaphores. Data moves between devices by JAX's collectives and lax.ppermute only.
A program may use at most 256 MiB of HBM per device.

v0:
```python
import jax
import jax.numpy as jnp
from jax import lax
from jax.sharding import PartitionSpec as P

GROUP = 128


def dequantize(codes, scales):
    spread = jnp.repeat(scales.astype(jnp.float32), GROUP, axis=1)
    return (codes.astype(jnp.float32) * spread).astype(jnp.bfloat16)


def on_device(tokens, w_codes, w_scale, gain, key_cot, value_cot, grad_scale):
    width = gain.shape[0]
    weight_piece = dequantize(
        lax.all_gather(w_codes, "node", axis=0, tiled=True),
        lax.all_gather(w_scale, "node", axis=0, tiled=True),
    )
    proj = jnp.dot(tokens, weight_piece, preferred_element_type=jnp.float32)
    proj, weight = (proj, weight_piece)
    key_raw = proj[:, :width]
    inverse = lax.rsqrt(jnp.mean(key_raw * key_raw, axis=-1, keepdims=True) + 1e-06)
    normed = key_raw * inverse
    keys = (normed * gain).astype(jnp.bfloat16)
    values = proj[:, width:].astype(jnp.bfloat16)
    upstream = key_cot.astype(jnp.float32) * gain
    key_grad = inverse * (upstream - normed * jnp.mean(upstream * normed, axis=-1, keepdims=True))
    grad_out = jnp.concatenate([key_grad.astype(jnp.bfloat16), value_cot], axis=1)
    gain_part = jnp.sum(key_cot.astype(jnp.float32) * normed, axis=0)
    product = lax.dot_general(
        tokens, grad_out, (((0,), (0,)), ((), ())), preferred_element_type=jnp.float32
    )
    coded = product / jnp.repeat(grad_scale, GROUP, axis=1)
    first = lax.psum_scatter(
        lax.optimization_barrier(coded.astype(jnp.bfloat16))
        .astype(jnp.float32)
        .astype(jnp.bfloat16),
        "node",
        scatter_dimension=0,
        tiled=True,
    ).astype(jnp.float32)
    first = lax.optimization_barrier(first.astype(jnp.bfloat16)).astype(jnp.float32)
    grad_codes = lax.psum_scatter(
        first.astype(jnp.bfloat16), "group", scatter_dimension=0, tiled=True
    ).astype(jnp.float32)
    grad_tokens = lax.dot_general(
        grad_out, weight, (((1,), (1,)), ((), ())), preferred_element_type=jnp.float32
    ).astype(jnp.bfloat16)
    grad_gain = lax.psum(gain_part, ("node", "group"))
    return (keys, values, grad_tokens, grad_codes, grad_gain)


def solution(mesh):
    in_specs = (
        P(("node", "group"), None),
        P("node", None),
        P("node", None),
        P(),
        P(("node", "group"), None),
        P(("node", "group"), None),
        P(),
    )
    out_specs = (
        P(("node", "group"), None),
        P(("node", "group"), None),
        P(("node", "group"), None),
        P(("node", "group"), None),
        P(),
    )
    return jax.shard_map(
        on_device, mesh=mesh, in_specs=in_specs, out_specs=out_specs, check_vma=False
    )
```

profile of v0, /device:TPU:1, one launch (start us, length us, event | category | flops | bytes accessed | tf_op | source)
XLA Modules:
  0.0 451.2 jit_solution(236356905981520854)
XLA Ops:
  7.2 0.7 all-gather.3.cloned.1.call-update
  8.0 2.3 copy.26
  10.3 1.2 copy.27
  11.4 27.3 %all-gather = bf16[16,320,16]{1,2,0:T(8,128)(2,1)S(1)} all-gather(bf16[1,320,16]{1,2,0:T(8,128)(2,1)S(1)} %bitcast.24), channel_id=1, replica_groups=mesh['node'=16,'group'=8] {'node'}, dimensions={0}, use_global_device_ids=true | all-gather | bytes 174080 | tf_op jit(solution)/shard_map/all_gather | solution.py:18
  38.7 0.4 copy.31
  39.2 105.0 %all-gather.3.cloned.1.call-done = bf16[5120,2048]{1,0:T(8,128)(2,1)} async-done(((bf16[320,2048]{1,0:T(8,128)(2,1)}), bf16[5120,2048]{1,0:T(8,128)(2,1)}) %all-gather.3.cloned.1.call-update) | async-done | bytes 20971536 | tf_op jit(solution)/shard_map/all_gather | solution.py:17
  144.2 20.7 %broadcast_in_dim.4 = f32[5120,16,128]{2,1,0:T(8,128)} broadcast(f32[5120,16]{1,0:T(8,128)S(1)} %bitcast.23), dimensions={0,1} | broadcast | bytes 42270720 | tf_op jit(solution)/shard_map/broadcast_in_dim | solution.py:10
  164.8 25.4 %convolution_bitcast_fusion = f32[384,2048]{0,1:T(8,128)S(1)} fusion(bf16[384,5120]{1,0:T(8,128)(2,1)S(1)} %copy-done, f32[640,8,16,128]{3,2,1,0:T(8,128)} %bitcast.21, bf16[5120,2048]{1,0:T(8,128)(2,1)} %all-gather.3.cloned.1.call-done), kind=kOutput, calls=%fused_computation.5 | convolution fusion | flops 8084520960 | bytes 69992448 | tf_op jit(solution)/shard_map/dot_general | solution.py:20
  190.5 0.7 fusion.7
  191.2 1.4 fusion.6
  192.5 0.9 copy-done.4
  193.4 17.5 %fusion.1 = bf16[5120,2048]{0,1:T(8,128)(2,1)} fusion(bf16[384,5120]{1,0:T(8,128)(2,1)} %param.7, f32[5120,16]{0,1:T(8,128)S(1)} %copy-done.9, bf16[384,1024]{0,1:T(8,128)(2,1)S(1)} %copy-done.2, bf16[384,1024]{0,1:T(8,128)(2,1)S(1)} %get-tuple-element.22), kind=kOutput, calls=%fused_computation.3 | convolution fusion | flops 8077180928 | bytes 26804224 | tf_op jit(solution)/shard_map/dot_general | solution.py:31
  210.9 28.0 %copy.32 = bf16[5120,2048]{1,0:T(8,128)(2,1)} copy(bf16[5120,2048]{0,1:T(8,128)(2,1)} %fusion.1) | data formatting | bytes 41943040
  239.0 1.0 slice.22
  239.9 2.3 copy.28
  242.2 2.3 copy.29
  244.5 66.9 %psum.7 = f32[1024]{0:T(1024)} all-reduce(f32[1024]{0:T(1024)S(1)} %get-tuple-element.20), channel_id=1, replica_groups=mesh['node'=16,'group'=8] {'node','group'}, use_global_device_ids=true, to_apply=%region_5.0 | all-reduce | flops 1024 | bytes 8192 | tf_op jit(solution)/shard_map/psum | solution.py:50
  311.4 94.2 %reduce-scatter.7.cloned.1.call-done = bf16[320,2048]{1,0:T(8,128)(2,1)} async-done(((bf16[5120,2048]{1,0:T(8,128)(2,1)}), bf16[320,2048]{1,0:T(8,128)(2,1)}) %reduce-scatter.7.cloned.1.call-update) | async-done | bytes 1310736
  405.6 1.8 copy.33
  407.4 1.6 copy.34
  409.1 31.7 %convolution_convert_fusion = bf16[384,5120]{1,0:T(8,128)(2,1)} fusion(bf16[384,1024]{0,1:T(8,128)(2,1)S(1)} %copy-done.3, bf16[384,1024]{0,1:T(8,128)(2,1)S(1)} %copy-done.5, f32[640,8,16,128]{3,2,1,0:T(8,128)} %bitcast.22, bf16[5120,2048]{1,0:T(8,128)(2,1)} %all-gather.3.cloned.1.call-done), kind=kOutput, calls=%fused_computation.4 | convolution fusion | flops 8089632768 | bytes 68419584 | tf_op jit(solution)/shard_map/dot_general | solution.py:47
  440.8 1.7 reduce-scatter.9.cloned.1.call-done
  442.5 1.2 copy.35
  443.7 0.9 copy.30
  (27 shorter events, 0.4 us)
Async XLA Ops:
  7.2 3.1 copy-start.6
  7.2 4.2 copy-start.8
  7.2 137.0 %all-gather.3.cloned.1.call-start = ((), (), s32[]{:S(2)}) async-start(), calls=%async_computation.2 | async-start | bytes 22282240 | tf_op jit(solution)/shard_map/all_gather | solution.py:17
  7.9 397.7 %reduce-scatter.7.cloned.1.call-start = ((), (), s32[]{:S(2)}) async-start(), calls=%async_computation.3 | async-start | bytes 22282240
  144.1 20.7 %copy-start = (bf16[384,5120]{1,0:T(8,128)(2,1)S(1)}, bf16[384,5120]{1,0:T(8,128)(2,1)}, u32[]{:S(2)}) copy-start(bf16[384,5120]{1,0:T(8,128)(2,1)} %param.7) | copy-start | bytes 11796484
  164.8 25.6 %copy-start.1 = (bf16[384,1024]{0,1:T(8,128)(2,1)S(1)}, bf16[384,1024]{0,1:T(8,128)(2,1)}, u32[]{:S(2)}) copy-start(bf16[384,1024]{0,1:T(8,128)(2,1)} %copy.26) | copy-start | bytes 2359300
  164.8 25.6 %copy-start.7 = (f32[1024]{0:T(1024)S(1)}, f32[1024]{0:T(1024)}, u32[]{:S(2)}) copy-start(f32[1024]{0:T(1024)} %param.10) | copy-start | bytes 12292
  190.4 3.0 copy-start.2
  190.5 3.0 copy-start.9
  192.5 0.9 copy-start.4
  238.9 203.6 %reduce-scatter.9.cloned.1.call-start = ((), (), s32[]{:S(2)}) async-start(), calls=%async_computation.4 | async-start | bytes 1474560
  311.4 97.6 %copy-start.3 = (bf16[384,1024]{0,1:T(8,128)(2,1)S(1)}, bf16[384,1024]{0,1:T(8,128)(2,1)}, u32[]{:S(2)}) copy-start(bf16[384,1024]{0,1:T(8,128)(2,1)} %copy.27) | copy-start | bytes 2359300
  311.4 97.6 %copy-start.5 = (bf16[384,1024]{0,1:T(8,128)(2,1)S(1)}, bf16[384,1024]{0,1:T(8,128)(2,1)}, u32[]{:S(2)}) copy-start(bf16[384,1024]{0,1:T(8,128)(2,1)} %copy-done.4) | copy-start | bytes 2359300
Sparse Core Ops, SparseCore 0:
  10.4 133.6 all-gather.2
  239.0 166.5 reduce-scatter.6
  409.2 33.3 reduce-scatter.8
where the time goes:
time: 456 us; the launch traced here: 451 us
  waiting for transfers between devices  202 us (44%)
  blocking collectives  94.2 us (21%)
  matrix products  74.6 us (16%)
  local copies, waits for them, and re-layouts  64.6 us (14%)
  between operations  13.9 us (3%)
    all_gather x1, waiting for transfers between devices, on_device(): lax.all_gather(w_codes, 'node', axis=0, tiled=True)  105 us
    unnamed x5, waiting for transfers between devices  96.6 us
    psum x1, blocking collectives, on_device(): grad_gain = lax.psum(gain_part, ('node', 'group'))  66.9 us
    unnamed x29, local copies, waits for them, and re-layouts  42.5 us
    dot_general x1, matrix products, on_device(): lax.dot_general(grad_out, weight, (((1,), (1,)), ((), ())), preferred_ele...  31.7 us
    all_gather x1, blocking collectives, on_device(): lax.all_gather(w_scale, 'node', axis=0, tiled=True)  27.3 us
    dot_general x1, matrix products, on_device(): proj = jnp.dot(tokens, weight_piece, preferred_element_type=jnp.float32)  25.4 us
    broadcast_in_dim x1, local copies, waits for them, and re-layouts, dequantize(): spread = jnp.repeat(scales.astype(jnp.float32), GROUP, axis=1)  20.7 us
  transfers between devices with their start and end apart: 3, of which 3 were waited for; matrix products, arithmetic and copies ran while one was open for 9% of the time, Pallas kernels for 0%

commit v1 on v0

v1 whole, which is shorter than its diff:
```python
import jax
import jax.numpy as jnp
from jax import lax
from jax.experimental import pallas as pl
from jax.experimental.pallas import tpu as pltpu
from jax.sharding import PartitionSpec as P

BF = jnp.bfloat16
F32 = jnp.float32
GROUP = 128
AXES = ("node", "group")
TOK = 384
ROWS = 320
SHARD = 640
D = 5120
KV = 1024
HALF = 512
QUART = 256
VMEM_LIMIT = 56 * 2**20


def coords(i):
    y, z_lo, core, x, z_hi = i % 4, (i // 4) % 2, (i // 8) % 2, (i // 16) % 4, i // 64
    return z_hi * 2 + z_lo, x, core, y


def flat(z, x, core, y):
    return (((z // 2 * 4 + x) * 2 + core) * 2 + z % 2) * 4 + y


def near(n, which):
    return n ^ 1 if which == 0 else 3 - n


def pairs_of(axis, step):
    out = []
    for i in range(128):
        z, x, core, y = coords(i)
        if axis == "core":
            out.append((i, flat(z, x, 1 - core, y)))
            continue
        which = step ^ core
        if axis == "x":
            out.append((i, flat(z, near(x, which), core, y)))
        if axis == "y":
            out.append((i, flat(z, x, core, near(y, which))))
        if axis == "z":
            out.append((i, flat(near(z, which), x, core, y)))
    return out


def pairs_zb():
    out = []
    for i in range(128):
        z, x, core, y = coords(i)
        out.append((i, flat(3 - z, x, core, y)))
    return out


def swap(v, axis, step=0):
    return lax.ppermute(v, AXES, pairs_of(axis, step))


def swap_zb(v):
    return lax.ppermute(v, AXES, pairs_zb())


def params():
    return pltpu.CompilerParams(vmem_limit_bytes=VMEM_LIMIT)


def cost(flops, nbytes):
    return pl.CostEstimate(flops=int(flops), bytes_accessed=int(nbytes), transcendentals=0)


def dequant_kernel(core_ref, own_ref, oth_ref, s_own_ref, s_oth_ref, ka, kb, va, vb):
    for c in (0, 1):

        @pl.when(core_ref[0] == c)
        def _():
            for r in (0, 1):
                codes = own_ref if r == c else oth_ref
                scale = s_own_ref if r == c else s_oth_ref
                for n, out in enumerate((ka, kb, va, vb)):
                    base = (n // 2) * 8 + c * 4 + (n % 2) * 2
                    for j in (0, 1):
                        b = base + j
                        out[r * ROWS : (r + 1) * ROWS, j * GROUP : (j + 1) * GROUP] = (
                            codes[:, b * GROUP : (b + 1) * GROUP].astype(F32)
                            * scale[:, b : b + 1].astype(F32)
                        ).astype(BF)


def dequant(core, own, oth, s_own, s_oth):
    vm = pl.BlockSpec(memory_space=pltpu.VMEM)
    return pl.pallas_call(
        dequant_kernel,
        grid_spec=pltpu.PrefetchScalarGridSpec(
            num_scalar_prefetch=1, grid=(), in_specs=[vm] * 4, out_specs=[vm] * 4
        ),
        out_shape=[jax.ShapeDtypeStruct((SHARD, QUART), BF)] * 4,
        compiler_params=params(),
        cost_estimate=cost(2e6, 4e6),
        name="dequant",
    )(core, own, oth, s_own, s_oth)


def dot(a, b):
    return jnp.dot(a, b, preferred_element_type=F32)


def fwd_early_kernel(ids, toa, tta, tob, ttb, wa, wb, out):
    @pl.when(pl.program_id(0) == 0)
    def _():
        out[...] = jnp.zeros_like(out)

    out[:TOK, :QUART] += dot(toa[...], wa[0])
    out[TOK:, :QUART] += dot(tta[...], wa[0])
    out[:TOK, QUART:] += dot(tob[...], wb[0])
    out[TOK:, QUART:] += dot(ttb[...], wb[0])


def tok_spec(offset):
    return pl.BlockSpec((TOK, SHARD), lambda j, ids: (0, ids[offset + j]))


def w_spec():
    return pl.BlockSpec((1, SHARD, QUART), lambda j, ids: (j, 0, 0))


def fwd_early(ids, t_own, t_oth, wa, wb):
    return pl.pallas_call(
        fwd_early_kernel,
        grid_spec=pltpu.PrefetchScalarGridSpec(
            num_scalar_prefetch=1,
            grid=(4,),
            in_specs=[tok_spec(0), tok_spec(0), tok_spec(4), tok_spec(4), w_spec(), w_spec()],
            out_specs=pl.BlockSpec((2 * TOK, HALF), lambda j, ids: (0, 0)),
        ),
        out_shape=jax.ShapeDtypeStruct((2 * TOK, HALF), F32),
        compiler_params=params(),
        cost_estimate=cost(2 * 768 * 2560 * 512, 12e6),
        name="key_projection_early",
    )(ids, t_own, t_oth, t_own, t_oth, wa, wb)


def fwd_late_kernel(ids, raw, toa, tta, tob, ttb, wa, wb, co, ct, gain, out, stats):
    @pl.when(pl.program_id(0) == 0)
    def _():
        out[...] = raw[...]

    out[:TOK, :QUART] += dot(toa[...], wa[0])
    out[TOK:, :QUART] += dot(tta[...], wa[0])
    out[:TOK, QUART:] += dot(tob[...], wb[0])
    out[TOK:, QUART:] += dot(ttb[...], wb[0])

    @pl.when(pl.program_id(0) == 3)
    def _():
        lane = lax.broadcasted_iota(jnp.int32, (TOK, GROUP), 1)
        for n, cot in enumerate((co, ct)):
            part = out[n * TOK : (n + 1) * TOK, :]
            square = jnp.sum(part * part, axis=1, keepdims=True)
            cross = jnp.sum(part * (cot[...].astype(F32) * gain[...]), axis=1, keepdims=True)
            stats[n * TOK : (n + 1) * TOK, :] = jnp.where(
                lane == 0, square, jnp.where(lane == 1, cross, 0.0)
            )


def fwd_late(ids, raw, t_own, t_oth, wa, wb, cot_own, cot_oth, gain):
    full = pl.BlockSpec((2 * TOK, HALF), lambda j, ids: (0, 0))
    cot = pl.BlockSpec((TOK, HALF), lambda j, ids: (0, ids[8]))
    return pl.pallas_call(
        fwd_late_kernel,
        grid_spec=pltpu.PrefetchScalarGridSpec(
            num_scalar_prefetch=1,
            grid=(4,),
            in_specs=[full, tok_spec(0), tok_spec(0), tok_spec(4), tok_spec(4), w_spec(), w_spec()]
            + [cot, cot, pl.BlockSpec((1, HALF), lambda j, ids: (0, ids[8]))],
            out_specs=[full, pl.BlockSpec((2 * TOK, GROUP), lambda j, ids: (0, 0))],
        ),
        out_shape=[
            jax.ShapeDtypeStruct((2 * TOK, HALF), F32),
            jax.ShapeDtypeStruct((2 * TOK, GROUP), F32),
        ],
        compiler_params=params(),
        cost_estimate=cost(2 * 768 * 2560 * 512, 14e6),
        name="key_projection_late",
    )(ids, raw, t_own, t_oth, t_own, t_oth, wa, wb, cot_own, cot_oth, gain)


def norm_kernel(ids, raw, mine, theirs, co, ct, gain, k_own, k_oth, g_own, g_oth, gsum):
    total = jnp.zeros((8, HALF), F32)
    for n, (cot, keys, grad) in enumerate(((co, k_own, g_own), (ct, k_oth, g_oth))):
        here = slice(n * TOK, (n + 1) * TOK)
        there = slice((1 - n) * TOK, (2 - n) * TOK)
        square = mine[here, 0:1] + theirs[there, 0:1]
        cross = mine[here, 1:2] + theirs[there, 1:2]
        inverse = lax.rsqrt(square * (1.0 / KV) + 1e-06)
        normed = raw[here, :] * inverse
        cotangent = cot[...].astype(F32)
        keys[...] = (normed * gain[...]).astype(BF)
        upstream = cotangent * gain[...]
        mean = cross * inverse * (1.0 / KV)
        grad[...] = (inverse * (upstream - normed * mean)).astype(BF)
        total += jnp.sum((cotangent * normed).reshape(TOK // 8, 8, HALF), axis=0)
    gsum[...] = jnp.broadcast_to(jnp.sum(total, axis=0, keepdims=True), (8, HALF))


def norm(ids, raw, mine, theirs, cot_own, cot_oth, gain):
    def whole(*shape):
        return pl.BlockSpec(shape, lambda j, ids: (0, 0))

    cot = pl.BlockSpec((TOK, HALF), lambda j, ids: (0, ids[8]))
    return pl.pallas_call(
        norm_kernel,
        grid_spec=pltpu.PrefetchScalarGridSpec(
            num_scalar_prefetch=1,
            grid=(1,),
            in_specs=[whole(2 * TOK, HALF), whole(2 * TOK, GROUP), whole(2 * TOK, GROUP)]
            + [cot, cot, pl.BlockSpec((1, HALF), lambda j, ids: (0, ids[8]))],
            out_specs=[whole(TOK, HALF)] * 4 + [whole(8, HALF)],
        ),
        out_shape=[jax.ShapeDtypeStruct((TOK, HALF), BF)] * 4
        + [jax.ShapeDtypeStruct((8, HALF), F32)],
        compiler_params=params(),
        cost_estimate=cost(8e6, 5e6),
        name="key_norm",
    )(ids, raw, mine, theirs, cot_own, cot_oth, gain)


def pick_early(w1, w2):
    return jnp.where(pl.program_id(0) < 4, w1[0], w2[0])


def pick_even(w1, w2):
    return jnp.where(pl.program_id(0) % 2 == 0, w1[0], w2[0])


def w_all_specs():
    first = pl.BlockSpec((1, SHARD, QUART), lambda j, ids: (jnp.minimum(j, 3), 0, 0))
    second = pl.BlockSpec((1, SHARD, QUART), lambda j, ids: (jnp.maximum(j - 4, 0), 0, 0))
    half = pl.BlockSpec((1, SHARD, QUART), lambda j, ids: (j // 2, 0, 0))
    return [first, second, half, half]


def fwd_value_kernel(ids, to, tt, a1, a2, b1, b2, v_own, v_oth, acc):
    wa, wb = pick_early(a1, a2), pick_even(b1, b2)

    @pl.when(pl.program_id(0) == 0)
    def _():
        acc[...] = jnp.zeros_like(acc)

    for n, tokens in enumerate((to, tt)):
        here = slice(n * TOK, (n + 1) * TOK)
        acc[here, :QUART] += dot(tokens[...], wa)
        acc[here, QUART:] += dot(tokens[...], wb)

    @pl.when(pl.program_id(0) == 7)
    def _():
        v_own[...] = acc[:TOK, :].astype(BF)
        v_oth[...] = acc[TOK:, :].astype(BF)


def fwd_value(ids, t_own, t_oth, weights):
    tok = pl.BlockSpec((TOK, SHARD), lambda j, ids: (0, ids[j]))
    out = pl.BlockSpec((TOK, HALF), lambda j, ids: (0, 0))
    return pl.pallas_call(
        fwd_value_kernel,
        grid_spec=pltpu.PrefetchScalarGridSpec(
            num_scalar_prefetch=1,
            grid=(8,),
            in_specs=[tok, tok] + w_all_specs(),
            out_specs=[out, out],
            scratch_shapes=[pltpu.VMEM((2 * TOK, HALF), F32)],
        ),
        out_shape=[jax.ShapeDtypeStruct((TOK, HALF), BF)] * 2,
        compiler_params=params(),
        cost_estimate=cost(2 * 768 * 5120 * 512, 14e6),
        name="value_projection",
    )(ids, t_own, t_oth, *weights)


def back(g_key, g_val, refs):
    ka = pick_early(refs[0], refs[1])
    kb = pick_even(refs[2], refs[3])
    va = pick_early(refs[4], refs[5])
    vb = pick_even(refs[6], refs[7])
    nt = (((1,), (1,)), ((), ()))
    total = lax.dot_general(g_key[:, :QUART], ka, nt, preferred_element_type=F32)
    total += lax.dot_general(g_key[:, QUART:], kb, nt, preferred_element_type=F32)
    total += lax.dot_general(g_val[:, :QUART], va, nt, preferred_element_type=F32)
    total += lax.dot_general(g_val[:, QUART:], vb, nt, preferred_element_type=F32)
    return total


def back_kernel(ids, g_key, g_val, *refs):
    refs[8][...] = back(g_key, g_val, refs).astype(BF)


def back_add_kernel(ids, g_key, g_val, *refs):
    refs[9][...] = (back(g_key, g_val, refs) + refs[8][...].astype(F32)).astype(BF)


def grad_tokens_of(ids, g_key, g_val, weights_k, weights_v, received=None):
    block = pl.BlockSpec((TOK, SHARD), lambda j, ids: (0, ids[j]))
    specs = [
        pl.BlockSpec((TOK, HALF), lambda j, ids: (0, 0)),
        pl.BlockSpec((TOK, HALF), lambda j, ids: (0, ids[8])),
    ]
    extra = [] if received is None else [received]
    return pl.pallas_call(
        back_kernel if received is None else back_add_kernel,
        grid_spec=pltpu.PrefetchScalarGridSpec(
            num_scalar_prefetch=1,
            grid=(8,),
            in_specs=specs + w_all_specs() * 2 + [block] * len(extra),
            out_specs=block,
        ),
        out_shape=jax.ShapeDtypeStruct((TOK, D), BF),
        compiler_params=params(),
        cost_estimate=cost(2 * 384 * 5120 * 1024, 16e6),
        name="token_gradient" if received is None else "token_gradient_sum",
    )(ids, g_key, g_val, *weights_k, *weights_v, *extra)


def codes_product(ids, to, tt, go, gt, scale, base, prod, width):
    tn = (((0,), (0,)), ((), ()))
    total = lax.dot_general(to[...], go[...], tn, preferred_element_type=F32)
    total += lax.dot_general(tt[...], gt[...], tn, preferred_element_type=F32)
    for j in range(width // GROUP):
        prod[:, j * GROUP : (j + 1) * GROUP] = (
            total[:, j * GROUP : (j + 1) * GROUP] / scale[:, base + j : base + j + 1]
        )


def piece(prod, offset):
    low = prod[pl.ds(pl.multiple_of(offset, 8), 40), :]
    high = prod[pl.ds(pl.multiple_of(offset + ROWS, 8), 40), :]
    return jnp.concatenate([low, high], axis=0).astype(BF)


def codes_y_kernel(base, width, ids, to, tt, go, gt, scale, keep, send, prod):
    codes_product(ids, to, tt, go, gt, scale, base, prod, width)
    k = pl.program_id(1)
    for m in (0, 1):
        z_slot = ids[8 + k * 2 + m]
        z_lo = ids[12 + m]
        for s in range(4):
            offset = z_lo * 160 + ids[14 + s] * 40
            out = keep if s < 2 else send
            out[s % 2, z_slot, 0] = piece(prod, offset)


def codes_x_kernel(base, width, ids, to, tt, go, gt, scale, keep, send, prod):
    codes_product(ids, to, tt, go, gt, scale, base, prod, width)
    k = pl.program_id(1)
    first = pl.program_id(0) < 2
    for m in (0, 1):
        z_slot = ids[8 + k * 2 + m]
        z_lo = ids[12 + m]
        for s in range(4):
            offset = z_lo * 160 + ids[14 + s] * 40
            value = piece(prod, offset)

            @pl.when(first)
            def _():
                send[0, s, z_slot] = value

            @pl.when(jnp.logical_not(first))
            def _():
                keep[0, s, z_slot] = value


def codes(kind, ids, t_own, t_oth, g_own, g_oth, scale, base, width, g_block):
    if kind == "y":
        order = lambda i: i
        shape = (2, 4, 4, 80, width)
        out_k = out_s = pl.BlockSpec((2, 4, 1, 80, width), lambda i, k, ids: (0, 0, i, 0, 0))
        body = codes_y_kernel
    else:
        order = lambda i: (i + 2) % 4
        shape = (2, 4, 4, 80, width)
        out_k = pl.BlockSpec((1, 4, 4, 80, width), lambda i, k, ids: (jnp.maximum(i - 2, 0), 0, 0, 0, 0))
        out_s = pl.BlockSpec((1, 4, 4, 80, width), lambda i, k, ids: (jnp.minimum(i, 1), 0, 0, 0, 0))
        body = codes_x_kernel
    tok = pl.BlockSpec((TOK, SHARD), lambda i, k, ids: (0, ids[order(i) * 2 + k]))
    grad = pl.BlockSpec((TOK, width), lambda i, k, ids: (0, g_block(ids)))
    return pl.pallas_call(
        lambda *refs: body(base, width, *refs),
        grid_spec=pltpu.PrefetchScalarGridSpec(
            num_scalar_prefetch=1,
            grid=(4, 2),
            in_specs=[tok, tok, grad, grad]
            + [pl.BlockSpec((SHARD, 8), lambda i, k, ids: (ids[order(i) * 2 + k], 0))],
            out_specs=[out_k, out_s],
            scratch_shapes=[pltpu.VMEM((SHARD, width), F32)],
        ),
        out_shape=[jax.ShapeDtypeStruct(shape, BF)] * 2,
        compiler_params=params(),
        cost_estimate=cost(2 * 768 * 5120 * width, 8e6 + 5120 * width * 2),
        name="weight_gradient_codes",
    )(ids, t_own, t_oth, g_own, g_oth, scale)


def f32(v):
    return v.astype(F32)


def reduce_axis(axis, keep, send):
    first = swap(send, axis, 0)
    second = swap((f32(keep[1]) + f32(first[1])).astype(BF), axis, 1)
    return f32(keep[0]) + f32(first[0]) + f32(second)


def reduce_all(order, keep, send):
    total = reduce_axis(order[0], keep, send)
    for axis in order[1:]:
        total = reduce_axis(axis, total[:2].astype(BF), total[2:].astype(BF))
    return total


def gather(ha, hb):
    g = swap_zb(ha)
    x1 = swap(hb, "x", 0)
    s1 = jnp.stack([ha, g])
    r1 = swap(s1, "x", 0)
    s2 = jnp.stack([hb, x1])
    q2 = swap(s2, "x", 1)
    c1 = jnp.concatenate([s1, r1])
    r2 = swap(c1, "x", 1)
    c2 = jnp.concatenate([s2, q2])
    rz = swap_zb(c2)
    return c1, r2, c2, rz


def on_device(tokens, w_codes, w_scale, gain, key_cot, value_cot, grad_scale):
    node, group = lax.axis_index("node"), lax.axis_index("group")
    z_hi, x, core = node // 8, (node // 2) % 4, node % 2
    z_lo, y = group // 4, group % 4
    z = z_hi * 2 + z_lo

    def ring(n):
        a, b = n ^ 1, 3 - n
        first, second = jnp.where(core == 0, a, b), jnp.where(core == 0, b, a)
        return [n, second, first, (n + 2) % 4]

    x_of, y_of, z_of = ring(x), ring(y), ring(z)
    gx = [x_of[0], x_of[2], x_of[1], x_of[3]]
    sid = {(dz, dx): (z_hi ^ dz) * 4 + gx[dx] for dz in (0, 1) for dx in range(4)}
    order = [(dz, dx) for dx in range(4) for dz in (0, 1)]
    as_ids = lambda values: jnp.stack([jnp.asarray(v, jnp.int32) for v in values])
    ids_all = as_ids([sid[o] for o in order] + [core])
    ids_early = as_ids([sid[o] for o in order[:4]] + [sid[(0, dx)] for dx in range(4)] + [core])
    ids_late = as_ids([sid[o] for o in order[4:]] + [sid[(1, dx)] for dx in range(4)] + [core])

    def slot_of(places, n):
        return sum(jnp.where(places[s] == n, s, 0) for s in range(4))

    z_slots = [slot_of(z_of, (z_hi ^ k) * 2 + (z_lo ^ m)) for k in (0, 1) for m in (0, 1)]
    ids_codes = as_ids(
        [(z_hi ^ k) * 4 + x_of[s] for s in range(4) for k in (0, 1)]
        + z_slots
        + [z_lo, z_lo ^ 1]
        + y_of
        + [core]
    )

    codes_oth = swap(w_codes, "core")
    scale_oth = swap(w_scale, "core")
    t_oth = swap(tokens, "core")
    vc_oth = swap(value_cot, "core")
    kc_oth = swap(key_cot, "core")
    core1 = as_ids([core])
    ka, kb, va, vb = dequant(core1, w_codes, codes_oth, w_scale, scale_oth)
    weights_k = gather(ka, kb)
    weights_v = gather(va, vb)

    scale_cols = jnp.concatenate(
        [
            lax.dynamic_slice_in_dim(grad_scale, core * 4, 4, axis=1),
            lax.dynamic_slice_in_dim(grad_scale, 8 + core * 4, 4, axis=1),
        ],
        axis=1,
    )
    v_keep, v_send = codes(
        "y", ids_codes, tokens, t_oth, value_cot, vc_oth, scale_cols, 4, HALF, lambda ids: ids[18]
    )
    sum_v = reduce_all(("y", "z", "x"), v_keep, v_send)

    gain2 = gain.reshape(1, KV)
    c1, r2, c2, rz = weights_k
    raw = fwd_early(ids_early, tokens, t_oth, c1, c2)
    raw, stats = fwd_late(ids_late, raw, tokens, t_oth, r2, rz, key_cot, kc_oth, gain2)
    stats_oth = swap(stats, "core")
    k_own, k_oth, g_own, g_oth, gsum = norm(ids_all, raw, stats, stats_oth, key_cot, kc_oth, gain2)

    a_keep, a_send = codes(
        "y", ids_codes, tokens, t_oth, g_own, g_oth, scale_cols, 0, QUART, lambda ids: 0
    )
    b_keep, b_send = codes(
        "x", ids_codes, tokens, t_oth, g_own, g_oth, scale_cols, 2, QUART, lambda ids: 1
    )
    sum_a = reduce_all(("y", "z", "x"), a_keep, a_send)
    sum_b = reduce_all(("x", "y", "z"), b_keep, b_send)

    for axis in ("x", "y", "z"):
        for step in (0, 1):
            gsum = gsum + swap(gsum, axis, step)
    gsum_oth = swap(gsum, "core")

    v_own, v_oth = fwd_value(ids_all, tokens, t_oth, weights_v)
    sent = grad_tokens_of(ids_all, g_oth, vc_oth, weights_k, weights_v)
    received = swap(sent, "core")
    grad_tokens = grad_tokens_of(ids_all, g_own, value_cot, weights_k, weights_v, received)

    def both(mine, theirs, axis):
        return jnp.where(
            core == 0,
            jnp.concatenate([mine, theirs], axis=axis),
            jnp.concatenate([theirs, mine], axis=axis),
        )

    keys = both(k_own, swap(k_oth, "core"), 1)
    values = both(v_own, swap(v_oth, "core"), 1)
    total = jnp.concatenate([sum_a, sum_b, sum_v], axis=1).reshape(2, 40, KV)
    mine = lax.dynamic_index_in_dim(total, core, 0, keepdims=False)
    theirs = swap(lax.dynamic_index_in_dim(total, 1 - core, 0, keepdims=False), "core")
    grad_codes = jnp.concatenate(
        [both(mine[:, :HALF], theirs[:, :HALF], 1), both(mine[:, HALF:], theirs[:, HALF:], 1)], axis=1
    )
    grad_gain = both(gsum[0], gsum_oth[0], 0)
    return (keys, values, grad_tokens, grad_codes, grad_gain)


def solution(mesh):
    rows = P(("node", "group"), None)
    in_specs = (rows, P("node", None), P("node", None), P(), rows, rows, P())
    out_specs = (rows, rows, rows, rows, P())
    return jax.shard_map(
        on_device, mesh=mesh, in_specs=in_specs, out_specs=out_specs, check_vma=False
    )
```

time: 456 us -> 263 us (0.58)
  waiting for transfers between devices: 202 us -> 74.1 us
  Pallas kernels: 0 us -> 99 us
  blocking collectives: 94.2 us -> 0 us
  matrix products: 74.6 us -> 0 us
  starting transfers between devices: 0.12 us -> 56.4 us
  local copies, waits for them, and re-layouts: 64.6 us -> 10.6 us
  other arithmetic: 2.22 us -> 20.2 us
  between operations: 13.9 us -> 1.27 us
    all_gather x1 -> x0, waiting for transfers between devices: 105 us -> none  [on_device(): lax.all_gather(w_codes, 'node', axis=0, tiled=True)]
    pallas_call x0 -> x10, Pallas kernels: none -> 99 us  [the longest x3 36.8 us: codes(): pl.pallas_call(lambda *refs: body(base, width, *refs), grid_spec=pltpu.Pr...]
    unnamed x5 -> x0, waiting for transfers between devices: 96.6 us -> none
    dot_general x3 -> x0, matrix products: 74.6 us -> none  [the longest x1 31.7 us: on_device(): lax.dot_general(grad_out, weight, (((1,), (1,)), ((), ())), preferred_ele...]
    ppermute x0 -> x47, waiting for transfers between devices: none -> 74.1 us  [the longest x43 63.5 us: swap(): return lax.ppermute(v, AXES, pairs_of(axis, step))]
    psum x1 -> x0, blocking collectives: 66.9 us -> none  [on_device(): grad_gain = lax.psum(gain_part, ('node', 'group'))]
    ppermute x0 -> x47, starting transfers between devices: none -> 56.4 us  [the longest x43 45.1 us: swap(): return lax.ppermute(v, AXES, pairs_of(axis, step))]
    unnamed x29 -> x51, local copies, waits for them, and re-layouts: 42.5 us -> 4.62 us
  transfers between devices with their start and end apart: 3 -> 47, of which waited for: 3 -> 22; matrix products, arithmetic and copies ran while one was open for 9% -> 10% of each run, Pallas kernels for 0% -> 38%
where the time goes in v1:
time: 263 us; the launch traced here: 262 us
  Pallas kernels  99 us (38%)
  waiting for transfers between devices  74.1 us (28%)
  starting transfers between devices  56.4 us (21%)
  other arithmetic  20.2 us (8%)
  local copies, waits for them, and re-layouts  10.6 us (4%)
    ppermute x43, waiting for transfers between devices, swap(): return lax.ppermute(v, AXES, pairs_of(axis, step))  63.5 us
    ppermute x43, starting transfers between devices, swap(): return lax.ppermute(v, AXES, pairs_of(axis, step))  45.1 us
    pallas_call x3, Pallas kernels, codes(): pl.pallas_call(lambda *refs: body(base, width, *refs), grid_spec=pltpu.Pr...  36.8 us
    pallas_call x2, Pallas kernels, grad_tokens_of(): pl.pallas_call(back_kernel if received is None else back_add_kernel, grid...  25.3 us
    pallas_call x1, Pallas kernels, fwd_value(): pl.pallas_call(fwd_value_kernel, grid_spec=pltpu.PrefetchScalarGridSpec(n...  12 us
    ppermute x4, starting transfers between devices, swap_zb(): return lax.ppermute(v, AXES, pairs_zb())  11.3 us
    ppermute x4, waiting for transfers between devices, swap_zb(): return lax.ppermute(v, AXES, pairs_zb())  10.6 us
    pallas_call x1, Pallas kernels, fwd_late(): pl.pallas_call(fwd_late_kernel, grid_spec=pltpu.PrefetchScalarGridSpec(nu...  9.49 us
  transfers between devices with their start and end apart: 47, of which 22 were waited for; matrix products, arithmetic and copies ran while one was open for 10% of the time, Pallas kernels for 38%

profile of v1, /device:TPU:1, one launch (start us, length us, event | category | flops | bytes accessed | tf_op | source)
XLA Modules:
  0.0 261.6 jit_solution(7657038354279429841)
XLA Ops:
  3.6 5.7 %collective-permute-done.2.s_oth_ref = bf16[320,16]{1,0:T(8,128)(2,1)S(1)} collective-permute-done((bf16[320,16]{1,0:T(8,128)(2,1)S(1)}, bf16[320,16]{1,0:T(8,128)(2,1)S(1)}, u32[]{:S(2)}, u32[]{:S(2)}) %collective-permute-start.2) | collective-permute-done | bytes 10272 | tf_op jit(solution)/shard_map/ppermute | solution.py:61
  11.7 3.3 %dequant.1 = (bf16[640,256]{1,0:T(8,128)(2,1)}, bf16[640,256]{1,0:T(8,128)(2,1)}, bf16[640,256]{1,0:T(8,128)(2,1)}, bf16[640,256]{1,0:T(8,128)(2,1)}) custom-call(s32[1]{0:T(128)} %bitcast.8.core_ref, bf16[320,2048]{1,0:T(8,128)(2,1)} %own_ref.1, bf16[320,2048]{1,0:T(8,128)(2,1)} %copy-done.16, bf16[320,16]{1,0:T(8,128)(2,1)} %copy-done.20, ...), custom_call_target="tpu_custom_call" | custom-call | flops 2000000 | bytes 4000000 | tf_op jit(solution)/shard_map/dequant/pallas_call | solution.py:96
  17.5 3.8 %collective-permute-start.3 = (bf16[640,256]{1,0:T(8,128)(2,1)}, bf16[640,256]{1,0:T(8,128)(2,1)S(1)}, u32[]{:S(2)}, u32[]{:S(2)}) collective-permute-start(bf16[640,256]{1,0:T(8,128)(2,1)} %get-tuple-element.24), channel_id=1, source_target_pairs={{0,68},{1,69},{2,70},{3,71},{4,64},{5,65},{6,66},{7,67},{8,76},{9,... | collective-permute-start | bytes 983048 | tf_op jit(solution)/shard_map/ppermute | solution.py:65
  24.6 5.1 %collective-permute-done.3 = bf16[640,256]{1,0:T(8,128)(2,1)S(1)} collective-permute-done((bf16[640,256]{1,0:T(8,128)(2,1)}, bf16[640,256]{1,0:T(8,128)(2,1)S(1)}, u32[]{:S(2)}, u32[]{:S(2)}) %collective-permute-start.3) | collective-permute-done | bytes 327712 | tf_op jit(solution)/shard_map/ppermute | solution.py:65
  30.6 5.5 %collective-permute-done.12 = bf16[640,256]{1,0:T(8,128)(2,1)S(1)} collective-permute-done((bf16[640,256]{1,0:T(8,128)(2,1)}, bf16[640,256]{1,0:T(8,128)(2,1)S(1)}, u32[]{:S(2)}, u32[]{:S(2)}) %collective-permute-start.12) | collective-permute-done | bytes 327712 | tf_op jit(solution)/shard_map/ppermute | solution.py:65
  42.8 3.8 %collective-permute-start.8 = (bf16[4,640,256]{2,1,0:T(8,128)(2,1)S(1)}, bf16[4,640,256]{2,1,0:T(8,128)(2,1)}, u32[]{:S(2)}, u32[]{:S(2)}) collective-permute-start(bf16[4,640,256]{2,1,0:T(8,128)(2,1)S(1)} %pad_maximum_fusion.1.wb.refs_2_), channel_id=1, source_target_pairs={{0,68},{1,69},{2,70},{3,71},{4,64},{5,65},{6,66},{7,67},{8,76},{9,... | collective-permute-start | bytes 3932168 | tf_op jit(solution)/shard_map/ppermute | solution.py:65
  47.8 8.1 %collective-permute-done.13 = bf16[2,640,256]{2,1,0:T(8,128)(2,1)} collective-permute-done((bf16[2,640,256]{2,1,0:T(8,128)(2,1)}, bf16[2,640,256]{2,1,0:T(8,128)(2,1)}, u32[]{:S(2)}, u32[]{:S(2)}) %collective-permute-start.13) | collective-permute-done | bytes 655392 | tf_op jit(solution)/shard_map/ppermute | solution.py:61
  69.6 7.9 %key_projection_early.1.raw = f32[768,512]{1,0:T(8,128)} custom-call(s32[9]{0:T(128)} %stack.144.ids, bf16[384,5120]{1,0:T(8,128)(2,1)} %refs_1_.5, bf16[384,5120]{1,0:T(8,128)(2,1)} %collective-permute-done.tta.ttb.tt.refs_2_, bf16[384,5120]{1,0:T(8,128)(2,1)} %refs_1_.5, bf16[384,5120]{1,0:T(8,128)(2,1)} %collective-permute-done.tta.ttb.tt.refs_2_, ...), custom_call_target="tpu_custom_call" | custom-call | flops 2013265920 | bytes 12000000 | tf_op jit(solution)/shard_map/key_projection_early/pallas_call | solution.py:132
  77.6 3.8 %collective-permute-start.17 = (bf16[4,640,256]{2,1,0:T(8,128)(2,1)}, bf16[4,640,256]{2,1,0:T(8,128)(2,1)}, u32[]{:S(2)}, u32[]{:S(2)}) collective-permute-start(bf16[4,640,256]{2,1,0:T(8,128)(2,1)} %pad_maximum_fusion.3.b1.refs_6_), channel_id=1, source_target_pairs={{0,68},{1,69},{2,70},{3,71},{4,64},{5,65},{6,66},{7,67},{8,76},{9,... | collective-permute-start | bytes 3932168 | tf_op jit(solution)/shard_map/ppermute | solution.py:65
  81.3 13.8 %weight_gradient_codes.5 = (bf16[2,4,4,80,512]{4,3,2,1,0:T(8,128)(2,1)}, bf16[2,4,4,80,512]{4,3,2,1,0:T(8,128)(2,1)}) custom-call(s32[19]{0:T(128)} %stack.167.refs_0_, bf16[384,5120]{1,0:T(8,128)(2,1)} %refs_1_.5, bf16[384,5120]{1,0:T(8,128)(2,1)} %collective-permute-done.tta.ttb.tt.refs_2_, bf16[384,1024]{1,0:T(8,128)(2,1)} %refs_3_.1, ...), custom_call_target="tpu_custom_call" | custom-call | flops 4026531840 | bytes 13242880 | tf_op jit(solution)/shard_map/weight_gradient_codes/pallas_call | solution.py:388
  97.9 9.5 %key_projection_late.1 = (f32[768,512]{1,0:T(8,128)}, f32[768,128]{1,0:T(8,128)}) custom-call(s32[9]{0:T(128)} %stack.143.ids, f32[768,512]{1,0:T(8,128)} %key_projection_early.1.raw, bf16[384,5120]{1,0:T(8,128)(2,1)} %refs_1_.5, bf16[384,5120]{1,0:T(8,128)(2,1)} %collective-permute-done.tta.ttb.tt.refs_2_, bf16[384,5120]{1,0:T(8,128)(2,1)} %refs_1_.5, ...), custom_call_target="tpu_custom_call" | custom-call | flops 2013265920 | bytes 14000000 | tf_op jit(solution)/shard_map/key_projection_late/pallas_call | solution.py:172
  110.1 4.2 %key_norm.1 = (bf16[384,512]{1,0:T(8,128)(2,1)}, bf16[384,512]{1,0:T(8,128)(2,1)}, bf16[384,512]{1,0:T(8,128)(2,1)}, bf16[384,512]{1,0:T(8,128)(2,1)}, f32[8,512]{1,0:T(8,128)}) custom-call(s32[9]{0:T(128)} %stack.142.ids, f32[768,512]{1,0:T(8,128)} %get-tuple-element.26.raw, f32[768,128]{1,0:T(8,128)} %get-tuple-element.27.mine, f32[768,128]{1,0:T(8,128)} %copy-done.17, ...), custom_call_target="tpu_custom_call" | custom-call | flops 8000000 | bytes 5000000 | tf_op jit(solution)/shard_map/key_norm/pallas_call | solution.py:214
  114.3 11.3 %weight_gradient_codes.3 = (bf16[2,4,4,80,256]{4,3,2,1,0:T(8,128)(2,1)}, bf16[2,4,4,80,256]{4,3,2,1,0:T(8,128)(2,1)}) custom-call(s32[19]{0:T(128)} %stack.167.refs_0_, bf16[384,5120]{1,0:T(8,128)(2,1)} %refs_1_.5, bf16[384,5120]{1,0:T(8,128)(2,1)} %collective-permute-done.tta.ttb.tt.refs_2_, bf16[384,512]{1,0:T(8,128)(2,1)} %get-tuple-element.34.g_key.refs_3_, ...), custom_call_target="tpu_custom_call" | custom-call | flops 2013265920 | bytes 10621440 | tf_op jit(solution)/shard_map/weight_gradient_codes/pallas_call | solution.py:388
  135.0 8.7 %collective-permute-done.42 = f32[8,512]{1,0:T(8,128)S(1)} collective-permute-done((f32[8,512]{1,0:T(8,128)S(1)}, f32[8,512]{1,0:T(8,128)S(1)}, u32[]{:S(2)}, u32[]{:S(2)}) %collective-permute-start.42) | collective-permute-done | bytes 16416 | tf_op jit(solution)/shard_map/ppermute | solution.py:61
  143.7 11.7 %weight_gradient_codes.4 = (bf16[2,4,4,80,256]{4,3,2,1,0:T(8,128)(2,1)}, bf16[2,4,4,80,256]{4,3,2,1,0:T(8,128)(2,1)}) custom-call(s32[19]{0:T(128)} %stack.167.refs_0_, bf16[384,5120]{1,0:T(8,128)(2,1)} %refs_1_.5, bf16[384,5120]{1,0:T(8,128)(2,1)} %collective-permute-done.tta.ttb.tt.refs_2_, bf16[384,512]{1,0:T(8,128)(2,1)} %get-tuple-element.34.g_key.refs_3_, ...), custom_call_target="tpu_custom_call" | custom-call | flops 2013265920 | bytes 10621440 | tf_op jit(solution)/shard_map/weight_gradient_codes/pallas_call | solution.py:388
  157.5 12.0 %value_projection.1 = (bf16[384,512]{1,0:T(8,128)(2,1)}, bf16[384,512]{1,0:T(8,128)(2,1)}) custom-call(s32[9]{0:T(128)} %stack.142.ids, bf16[384,5120]{1,0:T(8,128)(2,1)} %refs_1_.5, bf16[384,5120]{1,0:T(8,128)(2,1)} %collective-permute-done.tta.ttb.tt.refs_2_, bf16[4,640,256]{2,1,0:T(8,128)(2,1)} %pad_maximum_fusion.2.a1.refs_4_, ...), custom_call_target="tpu_custom_call" | custom-call | flops 4026531840 | bytes 14000000 | tf_op jit(solution)/shard_map/value_projection/pallas_call | solution.py:267
  172.3 12.2 %token_gradient.1 = bf16[384,5120]{1,0:T(8,128)(2,1)} custom-call(s32[9]{0:T(128)} %stack.142.ids, bf16[384,512]{1,0:T(8,128)(2,1)} %get-tuple-element.35.g_key.refs_4_, bf16[384,1024]{1,0:T(8,128)(2,1)} %collective-permute-done.19.g_val.refs_4_, bf16[4,640,256]{2,1,0:T(8,128)(2,1)} %copy-done.1, bf16[4,640,256]{2,1,0:T(8,128)(2,1)} %collective-permute-done.7.wa.refs_1_, ...), custom_call_target="tpu_custom_call" | custom-call | flops 4026531840 | bytes 16000000 | tf_op jit(solution)/shard_map/token_gradient/pallas_call | solution.py:311
  203.4 5.2 %collective-permute-done.29 = bf16[2,4,80,256]{3,2,1,0:T(8,128)(2,1)S(1)} collective-permute-done((bf16[2,4,80,256]{3,2,1,0:T(8,128)(2,1)S(1)}, bf16[2,4,80,256]{3,2,1,0:T(8,128)(2,1)S(1)}, u32[]{:S(2)}, u32[]{:S(2)}) %collective-permute-start.29) | collective-permute-done | bytes 327712 | tf_op jit(solution)/shard_map/ppermute | solution.py:61
  208.8 4.3 %collective-permute-done.34 = bf16[4,4,80,512]{3,2,1,0:T(8,128)(2,1)S(1)} collective-permute-done((bf16[4,4,80,512]{3,2,1,0:T(8,128)(2,1)S(1)}, bf16[4,4,80,512]{3,2,1,0:T(8,128)(2,1)S(1)}, u32[]{:S(2)}, u32[]{:S(2)}) %collective-permute-start.34) | collective-permute-done | bytes 1310752 | tf_op jit(solution)/shard_map/ppermute | solution.py:61
  220.8 5.1 %collective-permute-done.35 = bf16[2,4,80,512]{3,2,1,0:T(8,128)(2,1)S(1)} collective-permute-done((bf16[2,4,80,512]{3,2,1,0:T(8,128)(2,1)S(1)}, bf16[2,4,80,512]{3,2,1,0:T(8,128)(2,1)S(1)}, u32[]{:S(2)}, u32[]{:S(2)}) %collective-permute-start.35) | collective-permute-done | bytes 655392 | tf_op jit(solution)/shard_map/ppermute | solution.py:61
  227.7 4.4 %collective-permute-done.36 = bf16[4,80,512]{2,1,0:T(8,128)(2,1)S(1)} collective-permute-done((bf16[4,80,512]{2,1,0:T(8,128)(2,1)S(1)}, bf16[4,80,512]{2,1,0:T(8,128)(2,1)S(1)}, u32[]{:S(2)}, u32[]{:S(2)}) %collective-permute-start.36) | collective-permute-done | bytes 327712 | tf_op jit(solution)/shard_map/ppermute | solution.py:61
  233.6 4.1 %collective-permute-done.37 = bf16[2,80,512]{2,1,0:T(8,128)(2,1)S(1)} collective-permute-done((bf16[2,80,512]{2,1,0:T(8,128)(2,1)S(1)}, bf16[2,80,512]{2,1,0:T(8,128)(2,1)S(1)}, u32[]{:S(2)}, u32[]{:S(2)}) %collective-permute-start.37) | collective-permute-done | bytes 163872 | tf_op jit(solution)/shard_map/ppermute | solution.py:61
  239.8 13.0 %token_gradient_sum.1 = bf16[384,5120]{1,0:T(8,128)(2,1)} custom-call(s32[9]{0:T(128)} %stack.142.ids, bf16[384,512]{1,0:T(8,128)(2,1)} %get-tuple-element.34.g_key.refs_3_, bf16[384,1024]{1,0:T(8,128)(2,1)} %refs_3_.1, bf16[4,640,256]{2,1,0:T(8,128)(2,1)} %copy-done.1, bf16[4,640,256]{2,1,0:T(8,128)(2,1)} %collective-permute-done.7.wa.refs_1_, ...), custom_call_target="tpu_custom_call" | custom-call | flops 4026531840 | bytes 16000000 | tf_op jit(solution)/shard_map/token_gradient_sum/pallas_call | solution.py:311
  253.0 6.8 %collective-permute-start.39 = (f32[40,1024]{1,0:T(8,128)S(1)}, f32[40,1024]{1,0:T(8,128)S(1)}, u32[]{:S(2)}, u32[]{:S(2)}) collective-permute-start(f32[40,1024]{1,0:T(8,128)S(1)} %get-tuple-element.44), channel_id=1, source_target_pairs={{0,8},{1,9},{2,10},{3,11},{4,12},{5,13},{6,14},{7,15},{8,0},{9,1},... | collective-permute-start | bytes 491528 | tf_op jit(solution)/shard_map/ppermute | solution.py:61
  (187 shorter events, 87.0 us)
Async XLA Ops:
  0.6 69.0 %collective-permute-start = (bf16[384,5120]{1,0:T(8,128)(2,1)}, bf16[384,5120]{1,0:T(8,128)(2,1)}, u32[]{:S(2)}, u32[]{:S(2)}) collective-permute-start(bf16[384,5120]{1,0:T(8,128)(2,1)} %refs_1_.5), channel_id=1, source_target_pairs={{0,8},{1,9},{2,10},{3,11},{4,12},{5,13},{6,14},{7,15},{8,0},{9,1},... | collective-permute-start | bytes 11796488 | tf_op jit(solution)/shard_map/ppermute | solution.py:61
  17.5 12.2 %collective-permute-start.3 = (bf16[640,256]{1,0:T(8,128)(2,1)}, bf16[640,256]{1,0:T(8,128)(2,1)S(1)}, u32[]{:S(2)}, u32[]{:S(2)}) collective-permute-start(bf16[640,256]{1,0:T(8,128)(2,1)} %get-tuple-element.24), channel_id=1, source_target_pairs={{0,68},{1,69},{2,70},{3,71},{4,64},{5,65},{6,66},{7,67},{8,76},{9,... | collective-permute-start | bytes 983048 | tf_op jit(solution)/shard_map/ppermute | solution.py:65
  21.3 14.8 %collective-permute-start.12 = (bf16[640,256]{1,0:T(8,128)(2,1)}, bf16[640,256]{1,0:T(8,128)(2,1)S(1)}, u32[]{:S(2)}, u32[]{:S(2)}) collective-permute-start(bf16[640,256]{1,0:T(8,128)(2,1)} %get-tuple-element.30), channel_id=1, source_target_pairs={{0,68},{1,69},{2,70},{3,71},{4,64},{5,65},{6,66},{7,67},{8,76},{9,... | collective-permute-start | bytes 983048 | tf_op jit(solution)/shard_map/ppermute | solution.py:65
  21.3 15.9 %collective-permute-start.15 = (bf16[640,256]{1,0:T(8,128)(2,1)}, bf16[640,256]{1,0:T(8,128)(2,1)S(1)}, u32[]{:S(2)}, u32[]{:S(2)}) collective-permute-start(bf16[640,256]{1,0:T(8,128)(2,1)} %get-tuple-element.31), channel_id=1, source_target_pairs={{0,16},{1,17},{2,18},{3,19},{4,20},{5,21},{6,22},{7,23},{8,56},{9,... | collective-permute-start | bytes 983048 | tf_op jit(solution)/shard_map/ppermute | solution.py:61
  24.5 14.4 %collective-permute-start.6 = (bf16[2,640,256]{2,1,0:T(8,128)(2,1)}, bf16[2,640,256]{2,1,0:T(8,128)(2,1)S(1)}, u32[]{:S(2)}, u32[]{:S(2)}) collective-permute-start(bf16[2,640,256]{2,1,0:T(8,128)(2,1)} %pad_maximum_fusion.5), channel_id=1, source_target_pairs={{0,48},{1,49},{2,50},{3,51},{4,52},{5,53},{6,54},{7,55},{8,24},{9,... | collective-permute-start | bytes 1966088 | tf_op jit(solution)/shard_map/ppermute | solution.py:61
  30.6 12.2 %collective-permute-start.4 = (bf16[2,640,256]{2,1,0:T(8,128)(2,1)}, bf16[2,640,256]{2,1,0:T(8,128)(2,1)}, u32[]{:S(2)}, u32[]{:S(2)}) collective-permute-start(bf16[2,640,256]{2,1,0:T(8,128)(2,1)} %pad_maximum_fusion.4), channel_id=1, source_target_pairs={{0,16},{1,17},{2,18},{3,19},{4,20},{5,21},{6,22},{7,23},{8,56},{9,... | collective-permute-start | bytes 1966088 | tf_op jit(solution)/shard_map/ppermute | solution.py:61
  37.0 18.9 %collective-permute-start.13 = (bf16[2,640,256]{2,1,0:T(8,128)(2,1)}, bf16[2,640,256]{2,1,0:T(8,128)(2,1)}, u32[]{:S(2)}, u32[]{:S(2)}) collective-permute-start(bf16[2,640,256]{2,1,0:T(8,128)(2,1)} %pad_maximum_fusion.6), channel_id=1, source_target_pairs={{0,16},{1,17},{2,18},{3,19},{4,20},{5,21},{6,22},{7,23},{8,56},{9,... | collective-permute-start | bytes 1966088 | tf_op jit(solution)/shard_map/ppermute | solution.py:61
  37.3 40.3 %collective-permute-start.19 = (bf16[384,1024]{1,0:T(8,128)(2,1)}, bf16[384,1024]{1,0:T(8,128)(2,1)}, u32[]{:S(2)}, u32[]{:S(2)}) collective-permute-start(bf16[384,1024]{1,0:T(8,128)(2,1)} %refs_3_.1), channel_id=1, source_target_pairs={{0,8},{1,9},{2,10},{3,11},{4,12},{5,13},{6,14},{7,15},{8,0},{9,1},... | collective-permute-start | bytes 2359304 | tf_op jit(solution)/shard_map/ppermute | solution.py:61
  38.9 23.7 %collective-permute-start.16 = (bf16[2,640,256]{2,1,0:T(8,128)(2,1)}, bf16[2,640,256]{2,1,0:T(8,128)(2,1)}, u32[]{:S(2)}, u32[]{:S(2)}) collective-permute-start(bf16[2,640,256]{2,1,0:T(8,128)(2,1)} %pad_maximum_fusion.7), channel_id=1, source_target_pairs={{0,48},{1,49},{2,50},{3,51},{4,52},{5,53},{6,54},{7,55},{8,24},{9,... | collective-permute-start | bytes 1966088 | tf_op jit(solution)/shard_map/ppermute | solution.py:61
  42.8 55.1 %collective-permute-start.8 = (bf16[4,640,256]{2,1,0:T(8,128)(2,1)S(1)}, bf16[4,640,256]{2,1,0:T(8,128)(2,1)}, u32[]{:S(2)}, u32[]{:S(2)}) collective-permute-start(bf16[4,640,256]{2,1,0:T(8,128)(2,1)S(1)} %pad_maximum_fusion.1.wb.refs_2_), channel_id=1, source_target_pairs={{0,68},{1,69},{2,70},{3,71},{4,64},{5,65},{6,66},{7,67},{8,76},{9,... | collective-permute-start | bytes 3932168 | tf_op jit(solution)/shard_map/ppermute | solution.py:65
  55.9 42.1 %collective-permute-start.7 = (bf16[4,640,256]{2,1,0:T(8,128)(2,1)S(1)}, bf16[4,640,256]{2,1,0:T(8,128)(2,1)}, u32[]{:S(2)}, u32[]{:S(2)}) collective-permute-start(bf16[4,640,256]{2,1,0:T(8,128)(2,1)S(1)} %pad_maximum_fusion.wa.refs_0_), channel_id=1, source_target_pairs={{0,48},{1,49},{2,50},{3,51},{4,52},{5,53},{6,54},{7,55},{8,24},{9,... | collective-permute-start | bytes 3932168 | tf_op jit(solution)/shard_map/ppermute | solution.py:61
  62.7 32.4 %collective-permute-start.9 = (bf16[384,1024]{1,0:T(8,128)(2,1)S(1)}, bf16[384,1024]{1,0:T(8,128)(2,1)S(1)}, u32[]{:S(2)}, u32[]{:S(2)}) collective-permute-start(bf16[384,1024]{1,0:T(8,128)(2,1)S(1)} %copy-done.3), channel_id=1, source_target_pairs={{0,8},{1,9},{2,10},{3,11},{4,12},{5,13},{6,14},{7,15},{8,0},{9,1},... | collective-permute-start | bytes 2359304 | tf_op jit(solution)/shard_map/ppermute | solution.py:61
  69.6 87.8 %collective-permute-start.14 = (bf16[4,640,256]{2,1,0:T(8,128)(2,1)}, bf16[4,640,256]{2,1,0:T(8,128)(2,1)}, u32[]{:S(2)}, u32[]{:S(2)}) collective-permute-start(bf16[4,640,256]{2,1,0:T(8,128)(2,1)} %pad_maximum_fusion.2.a1.refs_4_), channel_id=1, source_target_pairs={{0,48},{1,49},{2,50},{3,51},{4,52},{5,53},{6,54},{7,55},{8,24},{9,... | collective-permute-start | bytes 3932168 | tf_op jit(solution)/shard_map/ppermute | solution.py:61
  77.6 79.9 %collective-permute-start.17 = (bf16[4,640,256]{2,1,0:T(8,128)(2,1)}, bf16[4,640,256]{2,1,0:T(8,128)(2,1)}, u32[]{:S(2)}, u32[]{:S(2)}) collective-permute-start(bf16[4,640,256]{2,1,0:T(8,128)(2,1)} %pad_maximum_fusion.3.b1.refs_6_), channel_id=1, source_target_pairs={{0,68},{1,69},{2,70},{3,71},{4,64},{5,65},{6,66},{7,67},{8,76},{9,... | collective-permute-start | bytes 3932168 | tf_op jit(solution)/shard_map/ppermute | solution.py:65
  95.1 92.3 %collective-permute-start.33 = (bf16[2,4,4,80,512]{4,3,2,1,0:T(8,128)(2,1)}, bf16[2,4,4,80,512]{4,3,2,1,0:T(8,128)(2,1)}, u32[]{:S(2)}, u32[]{:S(2)}) collective-permute-start(bf16[2,4,4,80,512]{4,3,2,1,0:T(8,128)(2,1)} %get-tuple-element.41), channel_id=1, source_target_pairs={{0,1},{1,0},{2,3},{3,2},{4,5},{5,4},{6,7},{7,6},{8,11},{9,10},{10,... | collective-permute-start | bytes 7864328 | tf_op jit(solution)/shard_map/ppermute | solution.py:61
  125.7 59.7 %collective-permute-start.21 = (bf16[2,4,4,80,256]{4,3,2,1,0:T(8,128)(2,1)}, bf16[2,4,4,80,256]{4,3,2,1,0:T(8,128)(2,1)S(1)}, u32[]{:S(2)}, u32[]{:S(2)}) collective-permute-start(bf16[2,4,4,80,256]{4,3,2,1,0:T(8,128)(2,1)} %get-tuple-element.37), channel_id=1, source_target_pairs={{0,1},{1,0},{2,3},{3,2},{4,5},{5,4},{6,7},{7,6},{8,11},{9,10},{10,... | collective-permute-start | bytes 3932168 | tf_op jit(solution)/shard_map/ppermute | solution.py:61
  155.4 30.3 %collective-permute-start.27 = (bf16[2,4,4,80,256]{4,3,2,1,0:T(8,128)(2,1)}, bf16[2,4,4,80,256]{4,3,2,1,0:T(8,128)(2,1)S(1)}, u32[]{:S(2)}, u32[]{:S(2)}) collective-permute-start(bf16[2,4,4,80,256]{4,3,2,1,0:T(8,128)(2,1)} %get-tuple-element.39), channel_id=1, source_target_pairs={{0,16},{1,17},{2,18},{3,19},{4,20},{5,21},{6,22},{7,23},{8,56},{9,... | collective-permute-start | bytes 3932168 | tf_op jit(solution)/shard_map/ppermute | solution.py:61
  157.4 13.0 %collective-permute-start.44 = (f32[8,512]{1,0:T(8,128)S(1)}, f32[8,512]{1,0:T(8,128)S(1)}, u32[]{:S(2)}, u32[]{:S(2)}) collective-permute-start(f32[8,512]{1,0:T(8,128)S(1)} %add.331), channel_id=1, source_target_pairs={{0,4},{1,5},{2,6},{3,7},{4,0},{5,1},{6,2},{7,3},{8,76},{9,77},{10,... | collective-permute-start | bytes 49160 | tf_op jit(solution)/shard_map/ppermute | solution.py:61
  169.5 19.8 %collective-permute-start.18 = (bf16[384,512]{1,0:T(8,128)(2,1)}, bf16[384,512]{1,0:T(8,128)(2,1)S(1)}, u32[]{:S(2)}, u32[]{:S(2)}) collective-permute-start(bf16[384,512]{1,0:T(8,128)(2,1)} %get-tuple-element.33), channel_id=1, source_target_pairs={{0,8},{1,9},{2,10},{3,11},{4,12},{5,13},{6,14},{7,15},{8,0},{9,1},... | collective-permute-start | bytes 1179656 | tf_op jit(solution)/shard_map/ppermute | solution.py:61
  170.5 14.0 %collective-permute-start.45 = (f32[8,512]{1,0:T(8,128)S(1)}, f32[8,512]{1,0:T(8,128)S(1)}, u32[]{:S(2)}, u32[]{:S(2)}) collective-permute-start(f32[8,512]{1,0:T(8,128)S(1)} %add.332), channel_id=1, source_target_pairs={{0,68},{1,69},{2,70},{3,71},{4,64},{5,65},{6,66},{7,67},{8,12},{9,... | collective-permute-start | bytes 49160 | tf_op jit(solution)/shard_map/ppermute | solution.py:61
  184.5 53.4 %collective-permute-start.20 = (bf16[384,5120]{1,0:T(8,128)(2,1)}, bf16[384,5120]{1,0:T(8,128)(2,1)S(1)}, u32[]{:S(2)}, u32[]{:S(2)}) collective-permute-start(bf16[384,5120]{1,0:T(8,128)(2,1)} %token_gradient.1), channel_id=1, source_target_pairs={{0,8},{1,9},{2,10},{3,11},{4,12},{5,13},{6,14},{7,15},{8,0},{9,1},... | collective-permute-start | bytes 11796488 | tf_op jit(solution)/shard_map/ppermute | solution.py:61
  189.3 23.7 %collective-permute-start.34 = (bf16[4,4,80,512]{3,2,1,0:T(8,128)(2,1)S(1)}, bf16[4,4,80,512]{3,2,1,0:T(8,128)(2,1)S(1)}, u32[]{:S(2)}, u32[]{:S(2)}) collective-permute-start(bf16[4,4,80,512]{3,2,1,0:T(8,128)(2,1)S(1)} %fusion.1), channel_id=1, source_target_pairs={{0,3},{1,2},{2,1},{3,0},{4,7},{5,6},{6,5},{7,4},{8,9},{9,8},{10,11... | collective-permute-start | bytes 3932168 | tf_op jit(solution)/shard_map/ppermute | solution.py:61
  203.3 12.5 %collective-permute-start.24 = (bf16[4,80,256]{2,1,0:T(8,128)(2,1)S(1)}, bf16[4,80,256]{2,1,0:T(8,128)(2,1)S(1)}, u32[]{:S(2)}, u32[]{:S(2)}) collective-permute-start(bf16[4,80,256]{2,1,0:T(8,128)(2,1)S(1)} %fusion.10), channel_id=1, source_target_pairs={{0,68},{1,69},{2,70},{3,71},{4,64},{5,65},{6,66},{7,67},{8,12},{9,... | collective-permute-start | bytes 491528 | tf_op jit(solution)/shard_map/ppermute | solution.py:61
  237.8 15.0 %collective-permute-start.38 = (bf16[80,512]{1,0:T(8,128)(2,1)S(1)}, bf16[80,512]{1,0:T(8,128)(2,1)S(1)}, u32[]{:S(2)}, u32[]{:S(2)}) collective-permute-start(bf16[80,512]{1,0:T(8,128)(2,1)S(1)} %fusion.12), channel_id=1, source_target_pairs={{0,48},{1,49},{2,50},{3,51},{4,52},{5,53},{6,54},{7,55},{8,24},{9,... | collective-permute-start | bytes 245768 | tf_op jit(solution)/shard_map/ppermute | solution.py:61
  (48 other events, 325.4 us)
